TPU v7x, 128 devices: a whole 4x4x4 slice. The times are simulated.
128 devices in a mesh: frames: 8 (over y_lo, x), rows: 16 (over z, y_hi, core).
Axes of the slice: x: 4, y: 4 (y_hi: 2, y_lo: 2; y = y_hi * 2 + y_lo), z: 4, core: 2. Of those that a mesh axis runs over, the one named last changes fastest.
Arguments:
- latents: bfloat16 [15360, 128], P(('frames', 'rows')), may hold values from -6 to 6
- conv_in_weight: bfloat16 [432, 384], replicated, may hold values from -0.3125 to 0.3125
- gain: float32 [384], replicated, may hold values from 0.1 to 1.9
- conv_mid_weight: bfloat16 [10368, 384], replicated, may hold values from -0.0625 to 0.0625
- up_weight: bfloat16 [3456, 192], replicated, may hold values from -0.109375 to 0.109375
Outputs:
- upsampled: bfloat16 [8, 192, 61440], P('frames', 'rows')
All inputs are finite; a program needn't handle non-finite values.
Results may differ from a plain program's by a relative error of at most 0.009.
Values may be sent and summed in bfloat16 or wider, within the bound.
A program may use at most 128 MiB of HBM per device.

v0:
```python
import functools

import jax
import jax.numpy as jnp
from jax import lax
from jax.experimental import pallas as pl
from jax.experimental.pallas import tpu as pltpu
from jax.sharding import PartitionSpec as P

F32 = jnp.float32
BF16 = jnp.bfloat16
MESH = pl.DeviceIdType.MESH
C = 384
C_UP = 192
BACK = 4
HALF = 80
TOKEN_ROW = 40


def peers():
    return [(k, d) for k in range(BACK + 1) for d in (-1, 0, 1) if (k, d) != (0, 0)]


def exchange_kernel(frames, rows, x_ref, t_ref, own, above, below, spread, send_sem, recv_sem):
    f, r = lax.axis_index("frames"), lax.axis_index("rows")

    def target_ok(k, d):
        return (f + k < frames) & (r + d >= 0) & (r + d < rows)

    def source_ok(k, d):
        return (f - k >= 0) & (r - d >= 0) & (r - d < rows)

    barrier = pltpu.get_barrier_semaphore()
    for k, d in peers():

        @pl.when(source_ok(k, d))
        def _(k=k, d=d):
            pl.semaphore_signal(barrier, inc=1, device_id=(f - k, r - d), device_id_type=MESH)

    def as_int(flag):
        return jnp.where(flag, 1, 0)

    sides = 1 + as_int(r > 0) + as_int(r < rows - 1)
    later = 1 + jnp.minimum(frames - 1 - f, BACK)
    pl.semaphore_wait(barrier, sides * later - 1)

    def copy(n, k, d):
        if d == 0:
            src, dst = x_ref, own.at[k - 1]
        elif d == 1:
            src, dst = x_ref.at[TOKEN_ROW:], above.at[k]
        else:
            src, dst = x_ref.at[: 2 * TOKEN_ROW], below.at[k]
        return pltpu.make_async_remote_copy(
            src_ref=src,
            dst_ref=dst,
            send_sem=send_sem.at[n],
            recv_sem=recv_sem.at[n],
            device_id=(f + k, r + d),
            device_id_type=MESH,
        )

    for n, (k, d) in enumerate(peers()):

        @pl.when(target_ok(k, d))
        def _(n=n, k=k, d=d):
            copy(n, k, d).start()

    lane = lax.broadcasted_iota(jnp.int32, (128, 512), 0)
    spot = lax.broadcasted_iota(jnp.int32, (128, 512), 1)
    column = 2 * (lane // 64) + (lane // 16) % 2
    window = (spot // 16) % 4 - column
    part = spot // 128
    wanted = jnp.where(part == 0, 1, jnp.where(part == 1, -1, jnp.where(part == 2, -3, 3)))
    same = ((lane // 32) % 2 == (spot // 64) % 2) & (lane % 16 == spot % 16)
    select = jnp.where(same & (window == wanted), 1.0, 0.0).astype(BF16)

    def unfold(block, h, first_row):
        count = block.shape[0]
        got = jnp.dot(block, select, preferred_element_type=F32)
        at = lax.broadcasted_iota(jnp.int32, (count, 128), 0) % TOKEN_ROW
        left = jnp.where(at == 0, 0.0, pltpu.roll(got[:, 256:384], 1, 0))
        right = jnp.where(at == TOKEN_ROW - 1, 0.0, pltpu.roll(got[:, 384:], count - 1, 0))
        spread[pl.ds(0, count, stride=2), :] = got[:, :128] + left
        spread[pl.ds(1, count, stride=2), :] = got[:, 128:256] + right
        t_ref[h, first_row * HALF : first_row * HALF + 2 * count, :] = spread[
            : 2 * count, :
        ].astype(BF16)

    unfold(x_ref[...], BACK, 2)
    for n, (k, d) in enumerate(peers()):
        dst = own.at[k - 1] if d == 0 else above.at[k] if d == 1 else below.at[k]
        ok = source_ok(k, d)

        @pl.when(ok)
        def _(n=n, k=k, d=d):
            copy(n, k, d).wait_recv()

        @pl.when(jnp.logical_not(ok))
        def _(dst=dst):
            dst[...] = jnp.zeros_like(dst)

        unfold(dst[...], BACK - k, 2 if d == 0 else 0 if d == 1 else 5)
    for n, (k, d) in enumerate(peers()):

        @pl.when(target_ok(k, d))
        def _(n=n, k=k, d=d):
            copy(n, k, d).wait_send()


def exchange(latents, frames, rows):
    n = len(peers())
    return pl.pallas_call(
        functools.partial(exchange_kernel, frames, rows),
        out_shape=jax.ShapeDtypeStruct((BACK + 1, 7 * HALF, 128), BF16),
        in_specs=[pl.BlockSpec(memory_space=pltpu.VMEM)],
        out_specs=pl.BlockSpec(memory_space=pltpu.VMEM),
        scratch_shapes=[
            pltpu.VMEM((BACK, 3 * TOKEN_ROW, 128), BF16),
            pltpu.VMEM((BACK + 1, 2 * TOKEN_ROW, 128), BF16),
            pltpu.VMEM((BACK + 1, 2 * TOKEN_ROW, 128), BF16),
            pltpu.VMEM((6 * TOKEN_ROW, 128), F32),
            pltpu.SemaphoreType.DMA((n,)),
            pltpu.SemaphoreType.DMA((n,)),
        ],
        compiler_params=pltpu.CompilerParams(
            collective_id=0, has_side_effects=True, vmem_limit_bytes=16 * 2**20
        ),
        name="exchange",
    )(latents)


def decode_kernel(
    rows,
    t_ref, gain_ref, w_in_ref, w_mid_hbm, w_up_hbm, o_ref,
    w_mid, w_up, w_first, w_phase, z, first, n0, n1, n1m, n0p, acc0, acc1, turned, sems,
):
    r = lax.axis_index("rows")
    top = jnp.where(r == 0, 0.0, 1.0)
    bottom = jnp.where(r == rows - 1, 0.0, 1.0)

    up_copy = pltpu.make_async_copy(w_up_hbm, w_up, sems.at[3])
    up_copy.start()
    mid_copies = [
        pltpu.make_async_copy(
            w_mid_hbm.at[a * 9 * C : (a + 1) * 9 * C], w_mid.at[a * 9 * C : (a + 1) * 9 * C], sems.at[a]
        )
        for a in range(3)
    ]
    for copy in mid_copies:
        copy.start()

    for a in range(3):
        for at, rho in enumerate((3, 0, 1, 2)):
            for kappa in range(4):
                start = a * 256 + at * 64 + kappa * 16
                for p in range(2):
                    for q in range(2):
                        b, e = rho - p, kappa - q
                        spot = (slice(start, start + 16), slice((2 * p + q) * C, (2 * p + q + 1) * C))
                        if 0 <= b <= 2 and 0 <= e <= 2:
                            tap = ((a * 3 + b) * 3 + e) * 16
                            w_first[spot] = w_in_ref[tap : tap + 16, :]
                        else:
                            w_first[spot] = jnp.zeros((16, C), BF16)

    lower = lax.broadcasted_iota(jnp.int32, (5 * HALF, 128), 1) < 64
    for h in range(BACK + 1):
        z[h, :, :128] = jnp.where(lower, t_ref[h, 2 * HALF :, :], t_ref[h, : 5 * HALF, :])
        z[h, :, 128:] = t_ref[h, HALF : 6 * HALF, :]

    gain = gain_ref[...]
    at = lax.broadcasted_iota(jnp.int32, (HALF, C), 0)

    def shifted_right(values):
        return jnp.where(at == 0, 0.0, pltpu.roll(values, 1, 0)).astype(BF16)

    def shifted_left(values):
        return jnp.where(at == HALF - 1, 0.0, pltpu.roll(values, HALF - 1, 0)).astype(BF16)

    def first_step(g, carry):
        block = jnp.concatenate([z[g], z[g + 1], z[g + 2]], axis=1)
        for p in range(2):
            result = jnp.dot(
                block, w_first[:, 2 * p * C : 2 * (p + 1) * C], preferred_element_type=F32
            )
            for w in range(5):
                row = 2 * w + p
                spot = slice(row * HALF, (row + 1) * HALF)
                for q in range(2):
                    rounded = result[w * HALF : (w + 1) * HALF, q * C : (q + 1) * C].astype(BF16)
                    first[q, spot, :] = rounded
                    value = rounded.astype(F32)
                    scale = lax.rsqrt(jnp.mean(value * value, axis=-1, keepdims=True) + 1e-6)
                    if row < 2:
                        scale = scale * top
                    if row >= 8:
                        scale = scale * bottom
                    value = value * scale * gain
                    value = value / (1.0 + jnp.exp(-value))
                    if q == 0:
                        n0[g, spot, :] = value.astype(BF16)
                        n0p[g, spot, :] = shifted_left(value)
                    else:
                        n1[g, spot, :] = value.astype(BF16)
                        n1m[g, spot, :] = shifted_right(value)
        return carry

    lax.fori_loop(0, 3, first_step, 0)

    up_copy.wait()
    met = (((0,), (1, 2)), ((0, 1), (2,)))
    for p in range(2):
        for q in range(2):
            for i in range(2):
                for j in range(2):
                    total = None
                    for b in met[p][i]:
                        for e in met[q][j]:
                            tap = (b * 3 + e) * C
                            term = w_up[tap : tap + C, :].astype(F32)
                            total = term if total is None else total + term
                    w_phase[2 * p + q, (2 * i + j) * C : (2 * i + j + 1) * C, :] = total.astype(BF16)

    for copy in mid_copies:
        copy.wait()

    M = 8 * HALF
    acc0[...] = jnp.zeros_like(acc0)
    acc1[...] = jnp.zeros_like(acc1)

    def mid_step(a, carry):
        base = a * 9 * C

        def tap(b, e):
            return w_mid[pl.ds(pl.multiple_of(base + (b * 3 + e) * C, C), C), :]

        def taken(*sources):
            return jnp.concatenate(
                [source[a, b * HALF : b * HALF + M, :] for b in range(3) for source in sources], axis=1
            )

        weight = jnp.concatenate(
            [
                jnp.concatenate([tap(b, 1 + k), tap(b, k)], axis=1)
                for b in range(3)
                for k in range(2)
            ],
            axis=0,
        )
        both = jnp.dot(taken(n0, n1), weight, preferred_element_type=F32)
        weight = jnp.concatenate([tap(b, 0) for b in range(3)], axis=0)
        acc0[...] += both[:, :C] + jnp.dot(taken(n1m), weight, preferred_element_type=F32)
        weight = jnp.concatenate([tap(b, 2) for b in range(3)], axis=0)
        acc1[...] += both[:, C:] + jnp.dot(taken(n0p), weight, preferred_element_type=F32)
        return carry

    lax.fori_loop(0, 3, mid_step, 0)

    for row in range(8):
        spot = slice(row * HALF, (row + 1) * HALF)
        source = slice((row + 1) * HALF, (row + 2) * HALF)
        for q, acc in enumerate((acc0, acc1)):
            value = acc[spot, :] + first[q, source, :].astype(F32)
            if row == 0:
                value = value * top
            if row == 7:
                value = value * bottom
            if q == 0:
                n0[0, spot, :] = value.astype(BF16)
                n0p[0, spot, :] = shifted_left(value)
            else:
                n1[0, spot, :] = value.astype(BF16)
                n1m[0, spot, :] = shifted_right(value)

    L = 6 * HALF
    columns = ((n1m, n0, n1), (n0, n1, n0p))
    for q in range(2):
        for p in range(2):
            halves = []
            for v in range(2):
                taken = jnp.concatenate(
                    [
                        source[0, (p + i) * HALF : (p + i) * HALF + L, :]
                        for i in range(2)
                        for source in columns[q][v : v + 2]
                    ],
                    axis=1,
                )
                halves.append(jnp.dot(taken, w_phase[2 * p + v], preferred_element_type=F32))
            whole = jnp.concatenate(halves, axis=1)
            for i in range(6):
                for t in range(3):
                    turned[pl.ds((q * 3 + t) * 16 + 2 * i + p, HALF, stride=96), :] = whole[
                        i * HALF : (i + 1) * HALF, t * 128 : (t + 1) * 128
                    ]

    def write(n, carry):
        for t in range(24):
            at_tile = n * 24 + t
            tile = turned[pl.ds(pl.multiple_of(at_tile * 16, 16), 16), :].astype(BF16)
            o_ref[0, :, pl.ds(pl.multiple_of(at_tile * 128, 128), 128)] = tile[:12, :]
        return carry

    lax.fori_loop(0, 20, write, 0)


def decode(tiles, gain, w_in, w_mid, w_up, rows):
    in_vmem = pl.BlockSpec(memory_space=pltpu.VMEM)
    in_hbm = pl.BlockSpec(memory_space=pl.ANY)
    return pl.pallas_call(
        functools.partial(decode_kernel, rows),
        out_shape=jax.ShapeDtypeStruct((1, 12, 2 * 160 * C_UP), BF16),
        in_specs=[in_vmem, in_vmem, in_vmem, in_hbm, in_hbm],
        out_specs=in_vmem,
        scratch_shapes=[
            pltpu.VMEM((27 * C, C), BF16),
            pltpu.VMEM((9 * C, C_UP), BF16),
            pltpu.VMEM((768, 4 * C), BF16),
            pltpu.VMEM((4, 4 * C, C_UP), BF16),
            pltpu.VMEM((BACK + 1, 5 * HALF, 256), BF16),
            pltpu.VMEM((2, 10 * HALF, C), BF16),
            *[pltpu.VMEM((3, 10 * HALF, C), BF16)] * 4,
            *[pltpu.VMEM((8 * HALF, C), F32)] * 2,
            pltpu.VMEM((160 * 3 * 16, 128), F32),
            pltpu.SemaphoreType.DMA((4,)),
        ],
        compiler_params=pltpu.CompilerParams(vmem_limit_bytes=60 * 2**20),
        name="decode",
    )(tiles, gain, w_in, w_mid, w_up)


def on_device(frames, rows, latents, conv_in_weight, gain, conv_mid_weight, up_weight):
    tiles = exchange(latents, frames, rows)
    return decode(tiles, gain.reshape(1, C), conv_in_weight, conv_mid_weight, up_weight, rows)


def solution(mesh):
    in_specs = (P(("frames", "rows"), None), P(), P(), P(), P())
    out_specs = P("frames", "rows", None)
    return jax.shard_map(
        functools.partial(on_device, mesh.shape["frames"], mesh.shape["rows"]),
        mesh=mesh,
        in_specs=in_specs,
        out_specs=out_specs,
        check_vma=False,
    )
```

profile of v0, /device:TPU:80, one launch (start us, length us, event | category | flops | bytes accessed | tf_op | source)
XLA Modules:
  0.0 47.1 jit_solution(10781930803145093797)
XLA Ops:
  0.0 1.2 %reshape.3.gain_ref = f32[1,384]{1,0:T(1,128)} reshape(f32[384]{0:T(512)} %param.7) | data formatting | bytes 3072 | tf_op jit(solution)/shard_map/reshape | solution.py:335
  1.2 0.0 copy-start.1
  1.3 0.8 %copy-done.1 = bf16[120,128]{1,0:T(8,128)(2,1)S(1)} copy-done((bf16[120,128]{1,0:T(8,128)(2,1)S(1)}, bf16[120,128]{1,0:T(8,128)(2,1)}, u32[]{:S(2)}) %copy-start.1) | copy-done | bytes 30744
  2.0 13.2 %exchange.1.t_ref = bf16[5,560,128]{2,1,0:T(8,128)(2,1)S(1)} custom-call(bf16[120,128]{1,0:T(8,128)(2,1)S(1)} %copy-done.1), custom_call_target="tpu_custom_call" | custom-call | tf_op jit(solution)/shard_map/exchange/pallas_call | solution.py:113
  15.3 0.0 copy-start
  15.3 0.8 %copy-done = bf16[5,560,128]{2,1,0:T(8,128)(2,1)} copy-done((bf16[5,560,128]{2,1,0:T(8,128)(2,1)}, bf16[5,560,128]{2,1,0:T(8,128)(2,1)S(1)}, u32[]{:S(2)}) %copy-start) | copy-done | bytes 716824
  16.1 3.7 %copy.6.w_up_hbm = bf16[3456,192]{1,0:T(8,128)(2,1)} copy(bf16[3456,192]{0,1:T(8,128)(2,1)} %param.9) | data formatting | bytes 2654208 | tf_op args[4]
  19.8 27.3 %decode.1 = bf16[1,12,61440]{2,1,0:T(8,128)(2,1)} custom-call(bf16[5,560,128]{2,1,0:T(8,128)(2,1)} %copy-done, f32[1,384]{1,0:T(1,128)} %reshape.3.gain_ref, bf16[432,384]{1,0:T(8,128)(2,1)} %w_in_ref.1, bf16[10368,384]{1,0:T(8,128)(2,1)} %w_mid_hbm.1, bf16[3456,192]{1,0:T(8,128)(2,1)} %copy.6.w_up_hbm), custom_call_target="tpu_custom_call" | custom-call | tf_op jit(solution)/shard_map/decode/pallas_call | solution.py:311
Async XLA Ops:
  1.2 0.8 %copy-start.1 = (bf16[120,128]{1,0:T(8,128)(2,1)S(1)}, bf16[120,128]{1,0:T(8,128)(2,1)}, u32[]{:S(2)}) copy-start(bf16[120,128]{1,0:T(8,128)(2,1)} %x_ref.1) | copy-start | bytes 92164
  15.3 0.9 %copy-start = (bf16[5,560,128]{2,1,0:T(8,128)(2,1)}, bf16[5,560,128]{2,1,0:T(8,128)(2,1)S(1)}, u32[]{:S(2)}) copy-start(bf16[5,560,128]{2,1,0:T(8,128)(2,1)S(1)} %exchange.1.t_ref) | copy-start | bytes 2150404
where the time goes:
time: 47.4 us; the launch traced here: 47.1 us
  Pallas kernels  40.6 us (86%)
  local copies, waits for them, and re-layouts  6.52 us (14%)
    pallas_call x1, Pallas kernels, decode(): pl.pallas_call(functools.partial(decode_kernel, rows), out_shape=jax.Shap...  27.3 us
    pallas_call x1, Pallas kernels, exchange(): pl.pallas_call(functools.partial(exchange_kernel, frames, rows), out_shap...  13.2 us
    unnamed x5, local copies, waits for them, and re-layouts  5.28 us
    reshape x1, local copies, waits for them, and re-layouts, on_device(): gain.reshape(1, C)  1.25 us

commit v1 on v0

v1 whole, which is shorter than its diff:
```python
import functools

import jax
import jax.numpy as jnp
from jax import lax
from jax.experimental import pallas as pl
from jax.experimental.pallas import tpu as pltpu
from jax.sharding import PartitionSpec as P

F32 = jnp.float32
BF16 = jnp.bfloat16
MESH = pl.DeviceIdType.MESH
C = 384
C_UP = 192
BACK = 4
HALF = 80
TOKEN_ROW = 40


def peers():
    return [(k, d) for k in range(BACK + 1) for d in (-1, 0, 1) if (k, d) != (0, 0)]


def dot_t(left, right):
    return lax.dot_general(left, right, (((1,), (1,)), ((), ())), preferred_element_type=F32)


def decode_kernel(
    frames, rows,
    x_ref, w_in_hbm, gain_hbm, w_mid_hbm, w_up_hbm,
    o_ref,
    mine, w_in, gain, w_mid, w_up, w_first, w_phase,
    own, above, below, spread, tiles, z, first, n0, n1, n1m, n0p, acc0, acc1, turned,
    send_sem, recv_sem, load_sem,
):
    f, r = lax.axis_index("frames"), lax.axis_index("rows")

    def target_ok(k, d):
        return (f + k < frames) & (r + d >= 0) & (r + d < rows)

    def source_ok(k, d):
        return (f - k >= 0) & (r - d >= 0) & (r - d < rows)

    loads = [
        pltpu.make_async_copy(source, target, load_sem.at[n])
        for n, (source, target) in enumerate(
            (
                (x_ref, mine),
                (w_in_hbm, w_in),
                (w_up_hbm, w_up),
                (gain_hbm, gain.at[0]),
                (w_mid_hbm, w_mid),
            )
        )
    ]
    for load in loads:
        load.start()
    barrier = pltpu.get_barrier_semaphore()
    for k, d in peers():

        @pl.when(source_ok(k, d))
        def _(k=k, d=d):
            pl.semaphore_signal(barrier, inc=1, device_id=(f - k, r - d), device_id_type=MESH)

    lane = lax.broadcasted_iota(jnp.int32, (128, 512), 0)
    spot = lax.broadcasted_iota(jnp.int32, (128, 512), 1)
    column = 2 * (lane // 64) + (lane // 16) % 2
    window = (spot // 16) % 4 - column
    part = spot // 128
    wanted = jnp.where(part == 0, 1, jnp.where(part == 1, -1, jnp.where(part == 2, -3, 3)))
    same = ((lane // 32) % 2 == (spot // 64) % 2) & (lane % 16 == spot % 16)
    select = jnp.where(same & (window == wanted), 1.0, 0.0).astype(BF16)

    for k, d in peers():
        dst = own.at[k - 1] if d == 0 else above.at[k] if d == 1 else below.at[k]

        @pl.when(jnp.logical_not(source_ok(k, d)))
        def _(dst=dst):
            dst[...] = jnp.zeros_like(dst)

    def as_int(flag):
        return jnp.where(flag, 1, 0)

    sides = 1 + as_int(r > 0) + as_int(r < rows - 1)
    later = 1 + jnp.minimum(frames - 1 - f, BACK)
    pl.semaphore_wait(barrier, sides * later - 1)

    def copy(n, k, d):
        if d == 0:
            src, dst = x_ref, own.at[k - 1]
        elif d == 1:
            src, dst = x_ref.at[TOKEN_ROW:], above.at[k]
        else:
            src, dst = x_ref.at[: 2 * TOKEN_ROW], below.at[k]
        return pltpu.make_async_remote_copy(
            src_ref=src,
            dst_ref=dst,
            send_sem=send_sem.at[n],
            recv_sem=recv_sem.at[n],
            device_id=(f + k, r + d),
            device_id_type=MESH,
        )

    for n, (k, d) in enumerate(peers()):

        @pl.when(target_ok(k, d))
        def _(n=n, k=k, d=d):
            copy(n, k, d).start()

    def unfold(block, h, first_row):
        count = block.shape[0]
        got = jnp.dot(block, select, preferred_element_type=F32)
        at = lax.broadcasted_iota(jnp.int32, (count, 128), 0) % TOKEN_ROW
        left = jnp.where(at == 0, 0.0, pltpu.roll(got[:, 256:384], 1, 0))
        right = jnp.where(at == TOKEN_ROW - 1, 0.0, pltpu.roll(got[:, 384:], count - 1, 0))
        spread[pl.ds(0, count, stride=2), :] = got[:, :128] + left
        spread[pl.ds(1, count, stride=2), :] = got[:, 128:256] + right
        tiles[h, first_row * HALF : first_row * HALF + 2 * count, :] = spread[
            : 2 * count, :
        ].astype(BF16)

    loads[1].wait()
    for a in range(3):
        for at, rho in enumerate((3, 0, 1, 2)):
            for kappa in range(4):
                start = a * 256 + at * 64 + kappa * 16
                for p in range(2):
                    for q in range(2):
                        b, e = rho - p, kappa - q
                        spot = (slice(start, start + 16), slice((2 * p + q) * C, (2 * p + q + 1) * C))
                        if 0 <= b <= 2 and 0 <= e <= 2:
                            tap = ((a * 3 + b) * 3 + e) * 16
                            w_first[spot] = w_in[tap : tap + 16, :]
                        else:
                            w_first[spot] = jnp.zeros((16, C), BF16)

    loads[2].wait()
    met = (((0,), (1, 2)), ((0, 1), (2,)))
    for p in range(2):
        for q in range(2):
            for i in range(2):
                for j in range(2):
                    total = None
                    for b in met[p][i]:
                        for e in met[q][j]:
                            tap = (b * 3 + e) * C
                            term = w_up[:, tap : tap + C].astype(F32)
                            total = term if total is None else total + term
                    w_phase[2 * p + q, :, (2 * i + j) * C : (2 * i + j + 1) * C] = total.astype(BF16)

    top = jnp.where(r == 0, 0.0, 1.0)
    bottom = jnp.where(r == rows - 1, 0.0, 1.0)

    lower = lax.broadcasted_iota(jnp.int32, (5 * HALF, 128), 1) < 64
    def arrive(frames_back):
        for n, (k, d) in enumerate(peers()):
            if k not in frames_back:
                continue

            @pl.when(source_ok(k, d))
            def _(n=n, k=k, d=d):
                copy(n, k, d).wait_recv()

            dst = own.at[k - 1] if d == 0 else above.at[k] if d == 1 else below.at[k]
            unfold(dst[...], BACK - k, 2 if d == 0 else 0 if d == 1 else 5)
        for k in frames_back:
            h = BACK - k
            z[h, :, :128] = jnp.where(lower, tiles[h, 2 * HALF :, :], tiles[h, : 5 * HALF, :])
            z[h, :, 128:] = tiles[h, HALF : 6 * HALF, :]

    loads[0].wait()
    unfold(mine[...], BACK, 2)

    loads[3].wait()
    half_gain = 0.5 * gain[...]
    at = lax.broadcasted_iota(jnp.int32, (HALF, C), 0)

    def shifted_right(values):
        return jnp.where(at == 0, 0.0, pltpu.roll(values, 1, 0)).astype(BF16)

    def shifted_left(values):
        return jnp.where(at == HALF - 1, 0.0, pltpu.roll(values, HALF - 1, 0)).astype(BF16)

    def first_step(g):
        block = jnp.concatenate([z[g], z[g + 1], z[g + 2]], axis=1)
        for p in range(2):
            result = jnp.dot(
                block, w_first[:, 2 * p * C : 2 * (p + 1) * C], preferred_element_type=F32
            )
            for w in range(5):
                row = 2 * w + p
                spot = slice(row * HALF, (row + 1) * HALF)
                for q in range(2):
                    rounded = result[w * HALF : (w + 1) * HALF, q * C : (q + 1) * C].astype(BF16)
                    if g == 2:
                        first[q, spot, :] = rounded
                    value = rounded.astype(F32)
                    scale = lax.rsqrt(jnp.mean(value * value, axis=-1, keepdims=True) + 1e-6)
                    if row < 2:
                        scale = scale * top
                    if row >= 8:
                        scale = scale * bottom
                    value = value * scale * half_gain
                    value = value + value * jnp.tanh(value)
                    if q == 0:
                        n0[g, spot, :] = value.astype(BF16)
                        n0p[g, spot, :] = shifted_left(value)
                    else:
                        n1[g, spot, :] = value.astype(BF16)
                        n1m[g, spot, :] = shifted_right(value)

    arrive((0, 1, 2))
    first_step(2)
    arrive((3,))
    first_step(1)
    arrive((4,))
    first_step(0)

    for load in loads[4:]:
        load.wait()

    M = 8 * HALF
    acc0[...] = jnp.zeros_like(acc0)
    acc1[...] = jnp.zeros_like(acc1)

    def mid_step(a, carry):
        base = a * 9 * C

        def tap(b, e):
            return w_mid[pl.ds(pl.multiple_of(base + (b * 3 + e) * C, C), C), :]

        def taken(*sources):
            return jnp.concatenate(
                [source[a, b * HALF : b * HALF + M, :] for b in range(3) for source in sources], axis=1
            )

        weight = jnp.concatenate(
            [
                jnp.concatenate([tap(b, 1 + k), tap(b, k)], axis=1)
                for b in range(3)
                for k in range(2)
            ],
            axis=0,
        )
        both = jnp.dot(taken(n0, n1), weight, preferred_element_type=F32)
        weight = jnp.concatenate([tap(b, 0) for b in range(3)], axis=0)
        acc0[...] += both[:, :C] + jnp.dot(taken(n1m), weight, preferred_element_type=F32)
        weight = jnp.concatenate([tap(b, 2) for b in range(3)], axis=0)
        acc1[...] += both[:, C:] + jnp.dot(taken(n0p), weight, preferred_element_type=F32)
        return carry

    lax.fori_loop(0, 3, mid_step, 0)

    for row in range(8):
        spot = slice(row * HALF, (row + 1) * HALF)
        source = slice((row + 1) * HALF, (row + 2) * HALF)
        for q, acc in enumerate((acc0, acc1)):
            value = acc[spot, :] + first[q, source, :].astype(F32)
            if row == 0:
                value = value * top
            if row == 7:
                value = value * bottom
            if q == 0:
                n0[0, spot, :] = value.astype(BF16)
                n0p[0, spot, :] = shifted_left(value)
            else:
                n1[0, spot, :] = value.astype(BF16)
                n1m[0, spot, :] = shifted_right(value)

    L = 6 * HALF
    columns = ((n1m, n0, n1), (n0, n1, n0p))
    for q in range(2):
        for p in range(2):
            halves = []
            for v in range(2):
                taken = jnp.concatenate(
                    [
                        source[0, (p + i) * HALF : (p + i) * HALF + L, :]
                        for i in range(2)
                        for source in columns[q][v : v + 2]
                    ],
                    axis=1,
                )
                halves.append(dot_t(taken, w_phase[2 * p + v]))
            whole = jnp.concatenate(halves, axis=1)
            for i in range(6):
                for t in range(3):
                    turned[pl.ds((q * 3 + t) * 16 + 2 * i + p, HALF, stride=96), :] = whole[
                        i * HALF : (i + 1) * HALF, t * 128 : (t + 1) * 128
                    ]

    def write(n, carry):
        tiles = turned[pl.ds(pl.multiple_of(n * 24 * 16, 16), 24 * 16), :].astype(BF16)
        whole = jnp.concatenate([tiles[t * 16 : t * 16 + 12, :] for t in range(24)], axis=1)
        o_ref[0, :, pl.ds(pl.multiple_of(n * 24 * 128, 128), 24 * 128)] = whole
        return carry

    lax.fori_loop(0, 20, write, 0)

    for n, (k, d) in enumerate(peers()):

        @pl.when(target_ok(k, d))
        def _(n=n, k=k, d=d):
            copy(n, k, d).wait_send()


def on_device(frames, rows, latents, conv_in_weight, gain, conv_mid_weight, up_weight):
    n = len(peers())
    return pl.pallas_call(
        functools.partial(decode_kernel, frames, rows),
        out_shape=jax.ShapeDtypeStruct((1, 12, 2 * 160 * C_UP), BF16),
        in_specs=[pl.BlockSpec(memory_space=pl.ANY)] * 5,
        out_specs=pl.BlockSpec(memory_space=pltpu.VMEM),
        scratch_shapes=[
            pltpu.VMEM((3 * TOKEN_ROW, 128), BF16),
            pltpu.VMEM((432, C), BF16),
            pltpu.VMEM((1, C), F32),
            pltpu.VMEM((27 * C, C), BF16),
            pltpu.VMEM((C_UP, 9 * C), BF16),
            pltpu.VMEM((768, 4 * C), BF16),
            pltpu.VMEM((4, C_UP, 4 * C), BF16),
            pltpu.VMEM((BACK, 3 * TOKEN_ROW, 128), BF16),
            pltpu.VMEM((BACK + 1, 2 * TOKEN_ROW, 128), BF16),
            pltpu.VMEM((BACK + 1, 2 * TOKEN_ROW, 128), BF16),
            pltpu.VMEM((6 * TOKEN_ROW, 128), F32),
            pltpu.VMEM((BACK + 1, 7 * HALF, 128), BF16),
            pltpu.VMEM((BACK + 1, 5 * HALF, 256), BF16),
            pltpu.VMEM((2, 10 * HALF, C), BF16),
            *[pltpu.VMEM((3, 10 * HALF, C), BF16)] * 4,
            *[pltpu.VMEM((8 * HALF, C), F32)] * 2,
            pltpu.VMEM((160 * 3 * 16, 128), F32),
            pltpu.SemaphoreType.DMA((n,)),
            pltpu.SemaphoreType.DMA((n,)),
            pltpu.SemaphoreType.DMA((5,)),
        ],
        compiler_params=pltpu.CompilerParams(
            collective_id=0, has_side_effects=True, vmem_limit_bytes=60 * 2**20
        ),
        name="decode",
    )(latents, conv_in_weight, gain, conv_mid_weight, up_weight.T)


def solution(mesh):
    in_specs = (P(("frames", "rows"), None), P(), P(), P(), P())
    out_specs = P("frames", "rows", None)
    return jax.shard_map(
        functools.partial(on_device, mesh.shape["frames"], mesh.shape["rows"]),
        mesh=mesh,
        in_specs=in_specs,
        out_specs=out_specs,
        check_vma=False,
    )
```

time: 47.4 us -> 41.5 us (0.88)
  the two profiles are of different devices: /device:TPU:80 before, /device:TPU:97 now
where the time goes in v1:
time: 41.5 us; the launch traced here: 41.4 us
  Pallas kernels  38.4 us (93%)
  local copies, waits for them, and re-layouts  2.94 us (7%)
    pallas_call x1, Pallas kernels, on_device(): pl.pallas_call(functools.partial(decode_kernel, frames, rows), out_shape=...  38.4 us
    unnamed x1, local copies, waits for them, and re-layouts  2.94 us

profile of v1, /device:TPU:97, one launch (start us, length us, event | category | flops | bytes accessed | tf_op | source)
XLA Modules:
  0.0 41.4 jit_solution(10537984680019548432)
XLA Ops:
  0.0 38.4 %decode.1 = bf16[1,12,61440]{2,1,0:T(8,128)(2,1)} custom-call(bf16[120,128]{1,0:T(8,128)(2,1)} %x_ref.1, bf16[432,384]{1,0:T(8,128)(2,1)} %w_in_hbm.1, f32[384]{0:T(512)} %gain_hbm.1, bf16[10368,384]{1,0:T(8,128)(2,1)} %w_mid_hbm.1, bf16[192,3456]{1,0:T(8,128)(2,1)} %bitcast.1), custom_call_target="tpu_custom_call" | custom-call | tf_op jit(solution)/shard_map/decode/pallas_call | solution.py:309
  38.4 2.9 %copy.7 = bf16[1,12,61440]{2,1,0:T(8,128)(2,1)} copy(bf16[1,12,61440]{2,1,0:T(8,128)(2,1)} %decode.1) | data formatting | bytes 2949120

commit v2 on v1

v2 whole, which is shorter than its diff:
```python
import functools

import jax
import jax.numpy as jnp
from jax import lax
from jax.experimental import pallas as pl
from jax.experimental.pallas import tpu as pltpu
from jax.sharding import PartitionSpec as P

F32 = jnp.float32
BF16 = jnp.bfloat16
MESH = pl.DeviceIdType.MESH
C = 384
C_UP = 192
BACK = 4
HALF = 80
MIX_LIMIT, UP_LIMIT = 58, 58
TOKEN_ROW = 40


def peers():
    return [(k, d) for k in range(BACK + 1) for d in (-1, 0, 1) if (k, d) != (0, 0)]


def dot_t(left, right):
    return lax.dot_general(left, right, (((1,), (1,)), ((), ())), preferred_element_type=F32)


def mix_kernel(
    frames, rows,
    x_ref, w_in_hbm, gain_hbm, w_mid_hbm, w_up_hbm,
    m0_hbm, m1_hbm, w_phase_hbm,
    mine, w_in, gain, w_mid, w_up, w_first, w_phase, w_pair, m0, m1,
    own, above, below, spread, tiles, z, first, n0, n1, result_a, result_b, sums,
    send_sem, recv_sem, load_sem, store_sem,
):
    f, r = lax.axis_index("frames"), lax.axis_index("rows")

    def target_ok(k, d):
        return (f + k < frames) & (r + d >= 0) & (r + d < rows)

    def source_ok(k, d):
        return (f - k >= 0) & (r - d >= 0) & (r - d < rows)

    loads = [
        pltpu.make_async_copy(source, target, load_sem.at[n])
        for n, (source, target) in enumerate(
            (
                (x_ref, mine),
                (w_in_hbm, w_in),
                (w_up_hbm, w_up),
                (gain_hbm, gain.at[0]),
                (w_mid_hbm, w_mid),
            )
        )
    ]
    for load in loads:
        load.start()
    barrier = pltpu.get_barrier_semaphore()
    for k, d in peers():

        @pl.when(source_ok(k, d))
        def _(k=k, d=d):
            pl.semaphore_signal(barrier, inc=1, device_id=(f - k, r - d), device_id_type=MESH)

    lane = lax.broadcasted_iota(jnp.int32, (128, 512), 0)
    spot = lax.broadcasted_iota(jnp.int32, (128, 512), 1)
    column = 2 * (lane // 64) + (lane // 16) % 2
    window = (spot // 16) % 4 - column
    part = spot // 128
    wanted = jnp.where(part == 0, 1, jnp.where(part == 1, -1, jnp.where(part == 2, -3, 3)))
    same = ((lane // 32) % 2 == (spot // 64) % 2) & (lane % 16 == spot % 16)
    select = jnp.where(same & (window == wanted), 1.0, 0.0).astype(BF16)

    for k, d in peers():
        dst = own.at[k - 1] if d == 0 else above.at[k] if d == 1 else below.at[k]

        @pl.when(jnp.logical_not(source_ok(k, d)))
        def _(dst=dst):
            dst[...] = jnp.zeros_like(dst)

    def as_int(flag):
        return jnp.where(flag, 1, 0)

    sides = 1 + as_int(r > 0) + as_int(r < rows - 1)
    later = 1 + jnp.minimum(frames - 1 - f, BACK)
    pl.semaphore_wait(barrier, sides * later - 1)

    def copy(n, k, d):
        if d == 0:
            src, dst = x_ref, own.at[k - 1]
        elif d == 1:
            src, dst = x_ref.at[TOKEN_ROW:], above.at[k]
        else:
            src, dst = x_ref.at[: 2 * TOKEN_ROW], below.at[k]
        return pltpu.make_async_remote_copy(
            src_ref=src,
            dst_ref=dst,
            send_sem=send_sem.at[n],
            recv_sem=recv_sem.at[n],
            device_id=(f + k, r + d),
            device_id_type=MESH,
        )

    for n, (k, d) in enumerate(peers()):

        @pl.when(target_ok(k, d))
        def _(n=n, k=k, d=d):
            copy(n, k, d).start()

    def unfold(block, h, first_row):
        count = block.shape[0]
        got = jnp.dot(block, select, preferred_element_type=F32)
        at = lax.broadcasted_iota(jnp.int32, (count, 128), 0) % TOKEN_ROW
        left = jnp.where(at == 0, 0.0, pltpu.roll(got[:, 256:384], 1, 0))
        right = jnp.where(at == TOKEN_ROW - 1, 0.0, pltpu.roll(got[:, 384:], count - 1, 0))
        spread[pl.ds(0, count, stride=2), :] = got[:, :128] + left
        spread[pl.ds(1, count, stride=2), :] = got[:, 128:256] + right
        for i in range(count // TOKEN_ROW):
            for iota in range(5):
                start = (first_row + i) * HALF + iota * 16
                tiles[h, start : start + 16, :] = spread[
                    pl.ds(i * HALF + iota, 16, stride=5), :
                ].astype(BF16)

    loads[1].wait()
    for a in range(3):
        for at, rho in enumerate((3, 0, 1, 2)):
            for kappa in range(4):
                start = a * 256 + at * 64 + kappa * 16
                for p in range(2):
                    for q in range(2):
                        b, e = rho - p, kappa - q
                        spot = (slice(start, start + 16), slice((2 * p + q) * C, (2 * p + q + 1) * C))
                        if 0 <= b <= 2 and 0 <= e <= 2:
                            tap = ((a * 3 + b) * 3 + e) * 16
                            w_first[spot] = w_in[tap : tap + 16, :]
                        else:
                            w_first[spot] = jnp.zeros((16, C), BF16)

    loads[2].wait()
    met = (((0,), (1, 2)), ((0, 1), (2,)))
    for p in range(2):
        for q in range(2):
            for i in range(2):
                for j in range(2):
                    total = None
                    for b in met[p][i]:
                        for e in met[q][j]:
                            tap = (b * 3 + e) * C
                            term = w_up[:, tap : tap + C].astype(F32)
                            total = term if total is None else total + term
                    w_phase[2 * p + q, :, (2 * i + j) * C : (2 * i + j + 1) * C] = total.astype(BF16)

    stores = [
        pltpu.make_async_copy(source, target, store_sem.at[n])
        for n, (source, target) in enumerate(((m0, m0_hbm), (m1, m1_hbm), (w_phase, w_phase_hbm)))
    ]
    stores[2].start()
    loads[4].wait()

    def pair_weight(n, carry):
        a, e = n // 3, n % 3
        for part in range(3):
            rows_of = [
                w_mid[pl.ds(pl.multiple_of(((a * 3 + b) * 3 + e) * C + part * 128, 128), 128), :].astype(F32)
                for b in range(3)
            ]
            outer = 0.5 * (rows_of[0] + rows_of[2])
            inner = 0.5 * rows_of[1]
            spot = pl.ds(pl.multiple_of((a * 3 + e) * C + part * 128, 128), 128)
            w_pair[0, spot, :] = (outer + inner).astype(BF16)
            w_pair[1, spot, :] = (outer - inner).astype(BF16)
        return carry

    lax.fori_loop(0, 9, pair_weight, 0)

    top = jnp.where(r == 0, 0.0, 1.0)
    bottom = jnp.where(r == rows - 1, 0.0, 1.0)

    lower = lax.broadcasted_iota(jnp.int32, (5 * HALF, 128), 1) < 64
    def arrive(frames_back):
        for n, (k, d) in enumerate(peers()):
            if k not in frames_back:
                continue

            @pl.when(source_ok(k, d))
            def _(n=n, k=k, d=d):
                copy(n, k, d).wait_recv()

            dst = own.at[k - 1] if d == 0 else above.at[k] if d == 1 else below.at[k]
            unfold(dst[...], BACK - k, 2 if d == 0 else 0 if d == 1 else 5)
        for k in frames_back:
            h = BACK - k
            z[h, :, :128] = jnp.where(lower, tiles[h, 2 * HALF :, :], tiles[h, : 5 * HALF, :])
            z[h, :, 128:] = tiles[h, HALF : 6 * HALF, :]

    loads[0].wait()
    unfold(mine[...], BACK, 2)

    loads[3].wait()
    half_gain = 0.5 * gain[...]
    at = lax.broadcasted_iota(jnp.int32, (16, C), 0)

    def shifted_right(values):
        return jnp.where(at == 0, 0.0, pltpu.roll(values, 1, 0)).astype(BF16)

    def shifted_left(values):
        return jnp.where(at == 15, 0.0, pltpu.roll(values, 15, 0)).astype(BF16)

    def put(target, spot, q, iota, value):
        start = (iota + q) * 16
        target[(*spot, slice(start, start + 16), slice(None))] = value.astype(BF16)
        if q == 0 and iota == 0:
            target[(*spot, slice(80, 96), slice(None))] = shifted_left(value)
        if q == 1 and iota == 4:
            target[(*spot, slice(0, 16), slice(None))] = shifted_right(value)

    def convolve(g, result):
        block = jnp.concatenate([z[g], z[g + 1], z[g + 2]], axis=1)
        for p in range(2):
            part = slice(2 * p * C, 2 * (p + 1) * C)
            result[:, part] = jnp.dot(block, w_first[:, part], preferred_element_type=F32)

    def normed(g, result, q, iota, row):
        w, p = row // 2, row % 2
        rounded = result[
            w * HALF + iota * 16 : w * HALF + (iota + 1) * 16, (2 * p + q) * C : (2 * p + q + 1) * C
        ].astype(BF16)
        if g == 2:
            first[q, row, iota * 16 : (iota + 1) * 16, :] = rounded
        value = rounded.astype(F32)
        scale = lax.rsqrt(jnp.mean(value * value, axis=-1, keepdims=True) + 1e-6)
        if row < 2:
            scale = scale * top
        if row >= 8:
            scale = scale * bottom
        value = value * scale * half_gain
        return value + value * jnp.tanh(value)

    def normalize(g, result):
        for q, target in enumerate((n0, n1)):
            for iota in range(5):
                even = normed(g, result, q, iota, 0)
                odd = normed(g, result, q, iota, 1)
                for pair in range(4):
                    next_even = normed(g, result, q, iota, 2 * pair + 2)
                    next_odd = normed(g, result, q, iota, 2 * pair + 3)
                    put(target, (g, 0, pair), q, iota, even - next_even)
                    put(target, (g, 1, pair), q, iota, odd + next_even)
                    put(target, (g, 2, pair), q, iota, next_even - odd)
                    put(target, (g, 3, pair), q, iota, odd - next_odd)
                    even, odd = next_even, next_odd

    arrive((0, 1, 2))
    convolve(2, result_a)
    arrive((3,))
    convolve(1, result_b)
    normalize(2, result_a)
    arrive((4,))
    convolve(0, result_a)
    normalize(1, result_b)
    normalize(0, result_a)

    def taken(views):
        return jnp.concatenate([view.reshape(4 * HALF, C) for view in views], axis=1)

    for k in range(4):

        def tap(a, e, k=k):
            if k == 0 or k == 3:
                start = ((a * 3 + 2 * (k // 3)) * 3 + e) * C
                return w_mid[start : start + C, :]
            start = (a * 3 + e) * C
            return w_pair[k - 1, start : start + C, :]

        weight = jnp.concatenate(
            [
                jnp.concatenate([tap(a, 1 + i), tap(a, i)], axis=1)
                for a in range(3)
                for i in range(2)
            ],
            axis=0,
        )
        views = [v for a in range(3) for v in (n0[a, k, :, :80, :], n1[a, k, :, 16:, :])]
        both = jnp.dot(taken(views), weight, preferred_element_type=F32)
        for q in range(2):
            weight = jnp.concatenate([tap(a, 2 * q) for a in range(3)], axis=0)
            views = [n0[a, k, :, 16:, :] if q == 1 else n1[a, k, :, :80, :] for a in range(3)]
            value = both[:, q * C : (q + 1) * C] + jnp.dot(
                taken(views), weight, preferred_element_type=F32
            )
            if k == 0:
                sums[0, q] = value
            elif k == 1:
                sums[0, q] += value
                sums[1, q] = value
            elif k == 2:
                sums[0, q] += value
                sums[1, q] -= value
            else:
                sums[1, q] -= value

    for q, target in enumerate((m0, m1)):
        for row in range(8):
            for iota in range(5):
                spot = slice((row // 2) * HALF + iota * 16, (row // 2) * HALF + (iota + 1) * 16)
                value = sums[row % 2, q, spot, :] + first[
                    q, row + 1, iota * 16 : (iota + 1) * 16, :
                ].astype(F32)
                if row == 0:
                    value = value * top
                if row == 7:
                    value = value * bottom
                put(target, (row,), q, iota, value)
        stores[q].start()

    for n, (k, d) in enumerate(peers()):

        @pl.when(target_ok(k, d))
        def _(n=n, k=k, d=d):
            copy(n, k, d).wait_send()
    for store in stores:
        store.wait()


def upsample_kernel(
    m0_hbm, m1_hbm, w_phase_hbm, o_ref, m0, m1, w_phase, turned, out, sems, load_sem
):
    loads = [
        pltpu.make_async_copy(m0_hbm, m0, load_sem.at[4]),
        pltpu.make_async_copy(m1_hbm, m1, load_sem.at[5]),
    ]
    phase_loads = [
        pltpu.make_async_copy(w_phase_hbm.at[n], w_phase.at[n], load_sem.at[n]) for n in range(4)
    ]
    for load in loads + phase_loads:
        load.start()
    for load in loads:
        load.wait()

    def piece(group, n):
        first_iota, count = group
        lanes = pl.ds(pl.multiple_of((n * 30 + first_iota * 6) * 128, 128), count * 6 * 128)
        sem = sems.at[n + (0 if first_iota == 0 else 16)]
        return pltpu.make_async_copy(out.at[:, :, lanes], o_ref.at[:, :, lanes], sem)

    groups = ((0, 3), (3, 2))
    for group in groups:
        first_iota, count = group
        size = count * 16
        plain = slice(first_iota * 16, first_iota * 16 + size)
        after = slice(first_iota * 16 + 16, first_iota * 16 + 16 + size)
        columns = (
            ((m1, plain), (m0, plain), (m1, after)),
            ((m0, plain), (m1, after), (m0, after)),
        )
        for q in range(2):
            for p in range(2):
                halves = []
                for v in range(2):
                    if first_iota == 0 and q == 0:
                        phase_loads[2 * p + v].wait()
                    taken = jnp.concatenate(
                        [
                            source[p + i : p + i + 6, spot, :].reshape(6 * size, C)
                            for i in range(2)
                            for source, spot in columns[q][v : v + 2]
                        ],
                        axis=1,
                    )
                    halves.append(dot_t(taken, w_phase[2 * p + v]))
                whole = jnp.concatenate(halves, axis=1)
                for i in range(6):
                    for at in range(count):
                        for t in range(3):
                            start = ((first_iota + at) * 6 + q * 3 + t) * 16 + 2 * i + p
                            turned[pl.ds(start, 16, stride=480), :] = whole[
                                i * size + at * 16 : i * size + (at + 1) * 16, t * 128 : (t + 1) * 128
                            ]

        def write(n, carry, group=group):
            first_iota, count = group
            for t in range(count * 6):
                tile = n * 30 + first_iota * 6 + t
                out[0, :, pl.ds(pl.multiple_of(tile * 128, 128), 128)] = turned[
                    pl.ds(pl.multiple_of(tile * 16, 16), 12), :
                ].astype(BF16)
            piece(group, n).start()
            return carry

        lax.fori_loop(0, 16, write, 0)

    for group in groups:

        def finish(n, carry, group=group):
            piece(group, n).wait()
            return carry

        lax.fori_loop(0, 16, finish, 0)


def upsample(m0, m1, w_phase):
    return pl.pallas_call(
        upsample_kernel,
        out_shape=jax.ShapeDtypeStruct((1, 12, 2 * 160 * C_UP), BF16),
        in_specs=[pl.BlockSpec(memory_space=pl.ANY)] * 3,
        out_specs=pl.BlockSpec(memory_space=pl.ANY),
        scratch_shapes=[
            *[pltpu.VMEM((8, 96, C), BF16)] * 2,
            pltpu.VMEM((4, C_UP, 4 * C), BF16),
            pltpu.VMEM((160 * 3 * 16, 128), F32),
            pltpu.VMEM((1, 12, 2 * 160 * C_UP), BF16),
            pltpu.SemaphoreType.DMA((32,)),
            pltpu.SemaphoreType.DMA((6,)),
        ],
        compiler_params=pltpu.CompilerParams(vmem_limit_bytes=UP_LIMIT * 2**20),
        name="upsample",
    )(m0, m1, w_phase)


def on_device(frames, rows, latents, conv_in_weight, gain, conv_mid_weight, up_weight):
    n = len(peers())
    m0, m1, w_phase = pl.pallas_call(
        functools.partial(mix_kernel, frames, rows),
        out_shape=[
            jax.ShapeDtypeStruct((8, 96, C), BF16),
            jax.ShapeDtypeStruct((8, 96, C), BF16),
            jax.ShapeDtypeStruct((4, C_UP, 4 * C), BF16),
        ],
        in_specs=[pl.BlockSpec(memory_space=pl.ANY)] * 5,
        out_specs=[pl.BlockSpec(memory_space=pl.ANY)] * 3,
        scratch_shapes=[
            pltpu.VMEM((3 * TOKEN_ROW, 128), BF16),
            pltpu.VMEM((432, C), BF16),
            pltpu.VMEM((1, C), F32),
            pltpu.VMEM((27 * C, C), BF16),
            pltpu.VMEM((C_UP, 9 * C), BF16),
            pltpu.VMEM((768, 4 * C), BF16),
            pltpu.VMEM((4, C_UP, 4 * C), BF16),
            pltpu.VMEM((2, 9 * C, C), BF16),
            *[pltpu.VMEM((8, 96, C), BF16)] * 2,
            pltpu.VMEM((BACK, 3 * TOKEN_ROW, 128), BF16),
            pltpu.VMEM((BACK + 1, 2 * TOKEN_ROW, 128), BF16),
            pltpu.VMEM((BACK + 1, 2 * TOKEN_ROW, 128), BF16),
            pltpu.VMEM((6 * TOKEN_ROW, 128), F32),
            pltpu.VMEM((BACK + 1, 7 * HALF, 128), BF16),
            pltpu.VMEM((BACK + 1, 5 * HALF, 256), BF16),
            pltpu.VMEM((2, 10, HALF, C), BF16),
            *[pltpu.VMEM((3, 4, 4, 96, C), BF16)] * 2,
            *[pltpu.VMEM((5 * HALF, 4 * C), F32)] * 2,
            pltpu.VMEM((2, 2, 4 * HALF, C), F32),
            pltpu.SemaphoreType.DMA((n,)),
            pltpu.SemaphoreType.DMA((n,)),
            pltpu.SemaphoreType.DMA((5,)),
            pltpu.SemaphoreType.DMA((3,)),
        ],
        compiler_params=pltpu.CompilerParams(
            collective_id=0, has_side_effects=True, vmem_limit_bytes=MIX_LIMIT * 2**20
        ),
        name="mix",
    )(latents, conv_in_weight, gain, conv_mid_weight, up_weight.T)
    return upsample(m0, m1, w_phase)


def solution(mesh):
    in_specs = (P(("frames", "rows"), None), P(), P(), P(), P())
    out_specs = P("frames", "rows", None)
    return jax.shard_map(
        functools.partial(on_device, mesh.shape["frames"], mesh.shape["rows"]),
        mesh=mesh,
        in_specs=in_specs,
        out_specs=out_specs,
        check_vma=False,
    )
```

time: 41.5 us -> 38.7 us (0.933)
  local copies, waits for them, and re-layouts: 2.94 us -> 0 us
    unnamed x1 -> x0, local copies, waits for them, and re-layouts: 2.94 us -> none
    pallas_call x1 -> x2, Pallas kernels: 38.4 us -> 38.4 us  [the longest x1 28.5 us: on_device(): pl.pallas_call(functools.partial(mix_kernel, frames, rows), out_shape=[ja...]
where the time goes in v2:
time: 38.7 us; the launch traced here: 38.6 us
  Pallas kernels  38.4 us (99%)
    pallas_call x1, Pallas kernels, on_device(): pl.pallas_call(functools.partial(mix_kernel, frames, rows), out_shape=[ja...  28.5 us
    pallas_call x1, Pallas kernels, upsample(): pl.pallas_call(upsample_kernel, out_shape=jax.ShapeDtypeStruct((1, 12, 2...  9.89 us

profile of v2, /device:TPU:97, one launch (start us, length us, event | category | flops | bytes accessed | tf_op | source)
XLA Modules:
  0.0 38.6 jit_solution(2901543629337299290)
XLA Ops:
  0.0 28.5 %mix.1 = (bf16[8,96,384]{2,1,0:T(8,128)(2,1)}, bf16[8,96,384]{2,1,0:T(8,128)(2,1)}, bf16[4,192,1536]{2,1,0:T(8,128)(2,1)}) custom-call(bf16[120,128]{1,0:T(8,128)(2,1)} %x_ref.1, bf16[432,384]{1,0:T(8,128)(2,1)} %w_in_hbm.1, f32[384]{0:T(512)} %gain_hbm.1, bf16[10368,384]{1,0:T(8,128)(2,1)} %w_mid_hbm.1, bf16[192,3456]{1,0:T(8,128)(2,1)} %bitcast.1), custom_call_target="tpu_custom_call" | custom-call | tf_op jit(solution)/shard_map/mix/pallas_call | solution.py:424
  28.6 9.9 %upsample.1 = bf16[1,12,61440]{2,1,0:T(8,128)(2,1)} custom-call(bf16[8,96,384]{2,1,0:T(8,128)(2,1)} %get-tuple-element.8.m0_hbm, bf16[8,96,384]{2,1,0:T(8,128)(2,1)} %get-tuple-element.9.m1_hbm, bf16[4,192,1536]{2,1,0:T(8,128)(2,1)} %get-tuple-element.10.w_phase_hbm), custom_call_target="tpu_custom_call" | custom-call | tf_op jit(solution)/shard_map/upsample/pallas_call | solution.py:404

commit v3 on v2

--- a/solution.py
+++ b/solution.py
@@ -14,6 +14,7 @@
 C_UP = 192
 BACK = 4
 HALF = 80
+PITCH = 481
 MIX_LIMIT, UP_LIMIT = 58, 58
 TOKEN_ROW = 40
 
@@ -79,6 +80,41 @@
         def _(dst=dst):
             dst[...] = jnp.zeros_like(dst)
 
+    loads[1].wait()
+    for a in range(3):
+        for at, rho in enumerate((3, 0, 1, 2)):
+            for kappa in range(4):
+                start = a * 256 + at * 64 + kappa * 16
+                for p in range(2):
+                    for q in range(2):
+                        b, e = rho - p, kappa - q
+                        spot = (slice(start, start + 16), slice((2 * p + q) * C, (2 * p + q + 1) * C))
+                        if 0 <= b <= 2 and 0 <= e <= 2:
+                            tap = ((a * 3 + b) * 3 + e) * 16
+                            w_first[spot] = w_in[tap : tap + 16, :]
+                        else:
+                            w_first[spot] = jnp.zeros((16, C), BF16)
+
+    loads[2].wait()
+    met = (((0,), (1, 2)), ((0, 1), (2,)))
+    for p in range(2):
+        for q in range(2):
+            for i in range(2):
+                for j in range(2):
+                    total = None
+                    for b in met[p][i]:
+                        for e in met[q][j]:
+                            tap = (b * 3 + e) * C
+                            term = w_up[:, tap : tap + C].astype(F32)
+                            total = term if total is None else total + term
+                    w_phase[2 * p + q, :, (2 * i + j) * C : (2 * i + j + 1) * C] = total.astype(BF16)
+
+    stores = [
+        pltpu.make_async_copy(source, target, store_sem.at[n])
+        for n, (source, target) in enumerate(((m0, m0_hbm), (m1, m1_hbm), (w_phase, w_phase_hbm)))
+    ]
+    stores[2].start()
+
     def as_int(flag):
         return jnp.where(flag, 1, 0)
 
@@ -123,40 +159,6 @@
                     pl.ds(i * HALF + iota, 16, stride=5), :
                 ].astype(BF16)
 
-    loads[1].wait()
-    for a in range(3):
-        for at, rho in enumerate((3, 0, 1, 2)):
-            for kappa in range(4):
-                start = a * 256 + at * 64 + kappa * 16
-                for p in range(2):
-                    for q in range(2):
-                        b, e = rho - p, kappa - q
-                        spot = (slice(start, start + 16), slice((2 * p + q) * C, (2 * p + q + 1) * C))
-                        if 0 <= b <= 2 and 0 <= e <= 2:
-                            tap = ((a * 3 + b) * 3 + e) * 16
-                            w_first[spot] = w_in[tap : tap + 16, :]
-                        else:
-                            w_first[spot] = jnp.zeros((16, C), BF16)
-
-    loads[2].wait()
-    met = (((0,), (1, 2)), ((0, 1), (2,)))
-    for p in range(2):
-        for q in range(2):
-            for i in range(2):
-                for j in range(2):
-                    total = None
-                    for b in met[p][i]:
-                        for e in met[q][j]:
-                            tap = (b * 3 + e) * C
-                            term = w_up[:, tap : tap + C].astype(F32)
-                            total = term if total is None else total + term
-                    w_phase[2 * p + q, :, (2 * i + j) * C : (2 * i + j + 1) * C] = total.astype(BF16)
-
-    stores = [
-        pltpu.make_async_copy(source, target, store_sem.at[n])
-        for n, (source, target) in enumerate(((m0, m0_hbm), (m1, m1_hbm), (w_phase, w_phase_hbm)))
-    ]
-    stores[2].start()
     loads[4].wait()
 
     def pair_weight(n, carry):
@@ -375,7 +377,7 @@
                     for at in range(count):
                         for t in range(3):
                             start = ((first_iota + at) * 6 + q * 3 + t) * 16 + 2 * i + p
-                            turned[pl.ds(start, 16, stride=480), :] = whole[
+                            turned[pl.ds(start, 16, stride=PITCH), :] = whole[
                                 i * size + at * 16 : i * size + (at + 1) * 16, t * 128 : (t + 1) * 128
                             ]
 
@@ -384,7 +386,7 @@
             for t in range(count * 6):
                 tile = n * 30 + first_iota * 6 + t
                 out[0, :, pl.ds(pl.multiple_of(tile * 128, 128), 128)] = turned[
-                    pl.ds(pl.multiple_of(tile * 16, 16), 12), :
+                    pl.ds(n * PITCH + (first_iota * 6 + t) * 16, 12), :
                 ].astype(BF16)
             piece(group, n).start()
             return carry
@@ -409,7 +411,7 @@
         scratch_shapes=[
             *[pltpu.VMEM((8, 96, C), BF16)] * 2,
             pltpu.VMEM((4, C_UP, 4 * C), BF16),
-            pltpu.VMEM((160 * 3 * 16, 128), F32),
+            pltpu.VMEM((16 * PITCH, 128), F32),
             pltpu.VMEM((1, 12, 2 * 160 * C_UP), BF16),
             pltpu.SemaphoreType.DMA((32,)),
             pltpu.SemaphoreType.DMA((6,)),

time: 38.7 us -> 37.2 us (0.961)
  Pallas kernels: 38.4 us -> 36.9 us
    pallas_call x1, Pallas kernels: 9.89 us -> 8.32 us  [upsample(): pl.pallas_call(upsample_kernel, out_shape=jax.ShapeDtypeStruct((1, 12, 2...]
where the time goes in v3:
time: 37.2 us; the launch traced here: 37 us
  Pallas kernels  36.9 us (99%)
    pallas_call x1, Pallas kernels, on_device(): pl.pallas_call(functools.partial(mix_kernel, frames, rows), out_shape=[ja...  28.5 us
    pallas_call x1, Pallas kernels, upsample(): pl.pallas_call(upsample_kernel, out_shape=jax.ShapeDtypeStruct((1, 12, 2...  8.32 us

profile of v3, /device:TPU:97, one launch (start us, length us, event | category | flops | bytes accessed | tf_op | source)
XLA Modules:
  0.0 37.0 jit_solution(17788464557651744061)
XLA Ops:
  0.0 28.5 %mix.1 = (bf16[8,96,384]{2,1,0:T(8,128)(2,1)}, bf16[8,96,384]{2,1,0:T(8,128)(2,1)}, bf16[4,192,1536]{2,1,0:T(8,128)(2,1)}) custom-call(bf16[120,128]{1,0:T(8,128)(2,1)} %x_ref.1, bf16[432,384]{1,0:T(8,128)(2,1)} %w_in_hbm.1, f32[384]{0:T(512)} %gain_hbm.1, bf16[10368,384]{1,0:T(8,128)(2,1)} %w_mid_hbm.1, bf16[192,3456]{1,0:T(8,128)(2,1)} %bitcast.1), custom_call_target="tpu_custom_call" | custom-call | tf_op jit(solution)/shard_map/mix/pallas_call | solution.py:426
  28.6 8.3 %upsample.1 = bf16[1,12,61440]{2,1,0:T(8,128)(2,1)} custom-call(bf16[8,96,384]{2,1,0:T(8,128)(2,1)} %get-tuple-element.8.m0_hbm, bf16[8,96,384]{2,1,0:T(8,128)(2,1)} %get-tuple-element.9.m1_hbm, bf16[4,192,1536]{2,1,0:T(8,128)(2,1)} %get-tuple-element.10.w_phase_hbm), custom_call_target="tpu_custom_call" | custom-call | tf_op jit(solution)/shard_map/upsample/pallas_call | solution.py:406

commit v4 on v3

--- a/solution.py
+++ b/solution.py
@@ -32,7 +32,7 @@
     x_ref, w_in_hbm, gain_hbm, w_mid_hbm, w_up_hbm,
     m0_hbm, m1_hbm, w_phase_hbm,
     mine, w_in, gain, w_mid, w_up, w_first, w_phase, w_pair, m0, m1,
-    own, above, below, spread, tiles, z, first, n0, n1, result_a, result_b, sums,
+    own, above, below, spread, tiles, z, first, n0, n1, result_a, result_b, result_c, sums,
     send_sem, recv_sem, load_sem, store_sem,
 ):
     f, r = lax.axis_index("frames"), lax.axis_index("rows")
@@ -110,10 +110,14 @@
                     w_phase[2 * p + q, :, (2 * i + j) * C : (2 * i + j + 1) * C] = total.astype(BF16)
 
     stores = [
-        pltpu.make_async_copy(source, target, store_sem.at[n])
-        for n, (source, target) in enumerate(((m0, m0_hbm), (m1, m1_hbm), (w_phase, w_phase_hbm)))
+        [
+            pltpu.make_async_copy(source.at[row], target.at[row], store_sem.at[q * 8 + row])
+            for row in range(8)
+        ]
+        for q, (source, target) in enumerate(((m0, m0_hbm), (m1, m1_hbm)))
     ]
-    stores[2].start()
+    phase_store = pltpu.make_async_copy(w_phase, w_phase_hbm, store_sem.at[16])
+    phase_store.start()
 
     def as_int(flag):
         return jnp.where(flag, 1, 0)
@@ -144,19 +148,25 @@
         def _(n=n, k=k, d=d):
             copy(n, k, d).start()
 
-    def unfold(block, h, first_row):
-        count = block.shape[0]
+    token = lax.broadcasted_iota(jnp.int32, (7 * TOKEN_ROW, 128), 0) % TOKEN_ROW
+
+    def unfold(k):
+        h = BACK - k
+        own_band = mine[...] if k == 0 else own[k - 1]
+        block = jnp.concatenate([above[k], below[k], own_band], axis=0)
         got = jnp.dot(block, select, preferred_element_type=F32)
-        at = lax.broadcasted_iota(jnp.int32, (count, 128), 0) % TOKEN_ROW
-        left = jnp.where(at == 0, 0.0, pltpu.roll(got[:, 256:384], 1, 0))
-        right = jnp.where(at == TOKEN_ROW - 1, 0.0, pltpu.roll(got[:, 384:], count - 1, 0))
-        spread[pl.ds(0, count, stride=2), :] = got[:, :128] + left
-        spread[pl.ds(1, count, stride=2), :] = got[:, 128:256] + right
-        for i in range(count // TOKEN_ROW):
+        left = jnp.where(token == 0, 0.0, pltpu.roll(got[:, 256:384], 1, 0))
+        right = jnp.where(token == TOKEN_ROW - 1, 0.0, pltpu.roll(got[:, 384:], 7 * TOKEN_ROW - 1, 0))
+        even, odd = got[:, :128] + left, got[:, 128:256] + right
+        for n, row in enumerate((0, 1, 5, 6, 2, 3, 4)):
+            part = slice(n * TOKEN_ROW, (n + 1) * TOKEN_ROW)
+            start = (h * 7 + row) * HALF
+            spread[pl.ds(start, TOKEN_ROW, stride=2), :] = even[part]
+            spread[pl.ds(start + 1, TOKEN_ROW, stride=2), :] = odd[part]
+        for row in range(7):
             for iota in range(5):
-                start = (first_row + i) * HALF + iota * 16
-                tiles[h, start : start + 16, :] = spread[
-                    pl.ds(i * HALF + iota, 16, stride=5), :
+                tiles[h, row * HALF + iota * 16 : row * HALF + (iota + 1) * 16, :] = spread[
+                    pl.ds((h * 7 + row) * HALF + iota, 16, stride=5), :
                 ].astype(BF16)
 
     loads[4].wait()
@@ -183,23 +193,19 @@
     lower = lax.broadcasted_iota(jnp.int32, (5 * HALF, 128), 1) < 64
     def arrive(frames_back):
         for n, (k, d) in enumerate(peers()):
-            if k not in frames_back:
-                continue
-
-            @pl.when(source_ok(k, d))
-            def _(n=n, k=k, d=d):
-                copy(n, k, d).wait_recv()
-
-            dst = own.at[k - 1] if d == 0 else above.at[k] if d == 1 else below.at[k]
-            unfold(dst[...], BACK - k, 2 if d == 0 else 0 if d == 1 else 5)
+            if k in frames_back:
+
+                @pl.when(source_ok(k, d))
+                def _(n=n, k=k, d=d):
+                    copy(n, k, d).wait_recv()
+
         for k in frames_back:
+            unfold(k)
             h = BACK - k
             z[h, :, :128] = jnp.where(lower, tiles[h, 2 * HALF :, :], tiles[h, : 5 * HALF, :])
             z[h, :, 128:] = tiles[h, HALF : 6 * HALF, :]
 
     loads[0].wait()
-    unfold(mine[...], BACK, 2)
-
     loads[3].wait()
     half_gain = 0.5 * gain[...]
     at = lax.broadcasted_iota(jnp.int32, (16, C), 0)
@@ -240,19 +246,20 @@
         value = value * scale * half_gain
         return value + value * jnp.tanh(value)
 
-    def normalize(g, result):
-        for q, target in enumerate((n0, n1)):
-            for iota in range(5):
-                even = normed(g, result, q, iota, 0)
-                odd = normed(g, result, q, iota, 1)
-                for pair in range(4):
-                    next_even = normed(g, result, q, iota, 2 * pair + 2)
-                    next_odd = normed(g, result, q, iota, 2 * pair + 3)
-                    put(target, (g, 0, pair), q, iota, even - next_even)
-                    put(target, (g, 1, pair), q, iota, odd + next_even)
-                    put(target, (g, 2, pair), q, iota, next_even - odd)
-                    put(target, (g, 3, pair), q, iota, odd - next_odd)
-                    even, odd = next_even, next_odd
+    def normalize(g, result, pieces=range(10)):
+        for piece in pieces:
+            q, iota = piece // 5, piece % 5
+            target = (n0, n1)[q]
+            even = normed(g, result, q, iota, 0)
+            odd = normed(g, result, q, iota, 1)
+            for pair in range(4):
+                next_even = normed(g, result, q, iota, 2 * pair + 2)
+                next_odd = normed(g, result, q, iota, 2 * pair + 3)
+                put(target, (g, 0, pair), q, iota, even - next_even)
+                put(target, (g, 1, pair), q, iota, odd + next_even)
+                put(target, (g, 2, pair), q, iota, next_even - odd)
+                put(target, (g, 3, pair), q, iota, odd - next_odd)
+                even, odd = next_even, next_odd
 
     arrive((0, 1, 2))
     convolve(2, result_a)
@@ -260,16 +267,14 @@
     convolve(1, result_b)
     normalize(2, result_a)
     arrive((4,))
-    convolve(0, result_a)
+    convolve(0, result_c)
     normalize(1, result_b)
-    normalize(0, result_a)
 
     def taken(views):
         return jnp.concatenate([view.reshape(4 * HALF, C) for view in views], axis=1)
 
-    for k in range(4):
-
-        def tap(a, e, k=k):
+    def accumulate(k, frames_of, fresh):
+        def tap(a, e):
             if k == 0 or k == 3:
                 start = ((a * 3 + 2 * (k // 3)) * 3 + e) * C
                 return w_mid[start : start + C, :]
@@ -279,50 +284,55 @@
         weight = jnp.concatenate(
             [
                 jnp.concatenate([tap(a, 1 + i), tap(a, i)], axis=1)
-                for a in range(3)
+                for a in frames_of
                 for i in range(2)
             ],
             axis=0,
         )
-        views = [v for a in range(3) for v in (n0[a, k, :, :80, :], n1[a, k, :, 16:, :])]
+        views = [v for a in frames_of for v in (n0[a, k, :, :80, :], n1[a, k, :, 16:, :])]
         both = jnp.dot(taken(views), weight, preferred_element_type=F32)
         for q in range(2):
-            weight = jnp.concatenate([tap(a, 2 * q) for a in range(3)], axis=0)
-            views = [n0[a, k, :, 16:, :] if q == 1 else n1[a, k, :, :80, :] for a in range(3)]
+            weight = jnp.concatenate([tap(a, 2 * q) for a in frames_of], axis=0)
+            views = [n0[a, k, :, 16:, :] if q == 1 else n1[a, k, :, :80, :] for a in frames_of]
             value = both[:, q * C : (q + 1) * C] + jnp.dot(
                 taken(views), weight, preferred_element_type=F32
             )
-            if k == 0:
-                sums[0, q] = value
-            elif k == 1:
-                sums[0, q] += value
-                sums[1, q] = value
-            elif k == 2:
-                sums[0, q] += value
-                sums[1, q] -= value
-            else:
-                sums[1, q] -= value
-
-    for q, target in enumerate((m0, m1)):
-        for row in range(8):
-            for iota in range(5):
-                spot = slice((row // 2) * HALF + iota * 16, (row // 2) * HALF + (iota + 1) * 16)
-                value = sums[row % 2, q, spot, :] + first[
-                    q, row + 1, iota * 16 : (iota + 1) * 16, :
-                ].astype(F32)
-                if row == 0:
-                    value = value * top
-                if row == 7:
-                    value = value * bottom
-                put(target, (row,), q, iota, value)
-        stores[q].start()
+            if k < 3:
+                sums[0, q] = value if fresh and k == 0 else sums[0, q] + value
+            if k > 0:
+                sums[1, q] = value if fresh and k == 1 else sums[1, q] + (value if k == 1 else -value)
+
+    def mix(parity):
+        for q, target in enumerate((m0, m1)):
+            for pair in range(4):
+                row = 2 * pair + parity
+                for iota in range(5):
+                    spot = slice(pair * HALF + iota * 16, pair * HALF + (iota + 1) * 16)
+                    value = sums[parity, q, spot, :] + first[
+                        q, row + 1, iota * 16 : (iota + 1) * 16, :
+                    ].astype(F32)
+                    if row == 0:
+                        value = value * top
+                    if row == 7:
+                        value = value * bottom
+                    put(target, (row,), q, iota, value)
+                stores[q][row].start()
+
+    for k, pieces in enumerate(((0, 1, 2), (3, 4, 5), (6, 7), (8, 9))):
+        accumulate(k, (1, 2), True)
+        normalize(0, result_c, pieces)
+    for k in range(3):
+        accumulate(k, (0,), False)
+    mix(0)
+    accumulate(3, (0,), False)
+    mix(1)
 
     for n, (k, d) in enumerate(peers()):
 
         @pl.when(target_ok(k, d))
         def _(n=n, k=k, d=d):
             copy(n, k, d).wait_send()
-    for store in stores:
+    for store in stores[0] + stores[1] + [phase_store]:
         store.wait()
 
 
@@ -445,17 +455,17 @@
             pltpu.VMEM((BACK, 3 * TOKEN_ROW, 128), BF16),
             pltpu.VMEM((BACK + 1, 2 * TOKEN_ROW, 128), BF16),
             pltpu.VMEM((BACK + 1, 2 * TOKEN_ROW, 128), BF16),
-            pltpu.VMEM((6 * TOKEN_ROW, 128), F32),
+            pltpu.VMEM(((BACK + 1) * 7 * HALF, 128), F32),
             pltpu.VMEM((BACK + 1, 7 * HALF, 128), BF16),
             pltpu.VMEM((BACK + 1, 5 * HALF, 256), BF16),
             pltpu.VMEM((2, 10, HALF, C), BF16),
             *[pltpu.VMEM((3, 4, 4, 96, C), BF16)] * 2,
-            *[pltpu.VMEM((5 * HALF, 4 * C), F32)] * 2,
+            *[pltpu.VMEM((5 * HALF, 4 * C), F32)] * 3,
             pltpu.VMEM((2, 2, 4 * HALF, C), F32),
             pltpu.SemaphoreType.DMA((n,)),
             pltpu.SemaphoreType.DMA((n,)),
             pltpu.SemaphoreType.DMA((5,)),
-            pltpu.SemaphoreType.DMA((3,)),
+            pltpu.SemaphoreType.DMA((17,)),
         ],
         compiler_params=pltpu.CompilerParams(
             collective_id=0, has_side_effects=True, vmem_limit_bytes=MIX_LIMIT * 2**20

time: 37.2 us -> 35.6 us (0.957)
  Pallas kernels: 36.9 us -> 35.3 us
    pallas_call x1, Pallas kernels: 28.5 us -> 27 us  [on_device(): pl.pallas_call(functools.partial(mix_kernel, frames, rows), out_shape=[ja...]
where the time goes in v4:
time: 35.6 us; the launch traced here: 35.5 us
  Pallas kernels  35.3 us (99%)
    pallas_call x1, Pallas kernels, on_device(): pl.pallas_call(functools.partial(mix_kernel, frames, rows), out_shape=[ja...  27 us
    pallas_call x1, Pallas kernels, upsample(): pl.pallas_call(upsample_kernel, out_shape=jax.ShapeDtypeStruct((1, 12, 2...  8.3 us

profile of v4, /device:TPU:97, one launch (start us, length us, event | category | flops | bytes accessed | tf_op | source)
XLA Modules:
  0.0 35.5 jit_solution(841054829276390310)
XLA Ops:
  0.0 27.0 %mix.1 = (bf16[8,96,384]{2,1,0:T(8,128)(2,1)}, bf16[8,96,384]{2,1,0:T(8,128)(2,1)}, bf16[4,192,1536]{2,1,0:T(8,128)(2,1)}) custom-call(bf16[120,128]{1,0:T(8,128)(2,1)} %x_ref.1, bf16[432,384]{1,0:T(8,128)(2,1)} %w_in_hbm.1, f32[384]{0:T(512)} %gain_hbm.1, bf16[10368,384]{1,0:T(8,128)(2,1)} %w_mid_hbm.1, bf16[192,3456]{1,0:T(8,128)(2,1)} %bitcast.1), custom_call_target="tpu_custom_call" | custom-call | tf_op jit(solution)/shard_map/mix/pallas_call | solution.py:436
  27.0 8.3 %upsample.1 = bf16[1,12,61440]{2,1,0:T(8,128)(2,1)} custom-call(bf16[8,96,384]{2,1,0:T(8,128)(2,1)} %get-tuple-element.8.m0_hbm, bf16[8,96,384]{2,1,0:T(8,128)(2,1)} %get-tuple-element.9.m1_hbm, bf16[4,192,1536]{2,1,0:T(8,128)(2,1)} %get-tuple-element.10.w_phase_hbm), custom_call_target="tpu_custom_call" | custom-call | tf_op jit(solution)/shard_map/upsample/pallas_call | solution.py:416

commit v5 on v4

--- a/solution.py
+++ b/solution.py
@@ -97,17 +97,20 @@
 
     loads[2].wait()
     met = (((0,), (1, 2)), ((0, 1), (2,)))
-    for p in range(2):
-        for q in range(2):
-            for i in range(2):
-                for j in range(2):
-                    total = None
-                    for b in met[p][i]:
-                        for e in met[q][j]:
-                            tap = (b * 3 + e) * C
-                            term = w_up[:, tap : tap + C].astype(F32)
-                            total = term if total is None else total + term
-                    w_phase[2 * p + q, :, (2 * i + j) * C : (2 * i + j + 1) * C] = total.astype(BF16)
+    for v in range(2):
+        for j in range(2):
+            spot = slice(j * C, (j + 1) * C)
+            by_row = []
+            for b in range(3):
+                total = None
+                for e in met[v][j]:
+                    tap = (b * 3 + e) * C
+                    term = w_up[:, tap : tap + C].astype(F32)
+                    total = term if total is None else total + term
+                by_row.append(total)
+            w_phase[v, :, spot] = (by_row[0] + by_row[1] + by_row[2]).astype(BF16)
+            w_phase[2 + v, :, spot] = (-by_row[0]).astype(BF16)
+            w_phase[4 + v, :, spot] = by_row[2].astype(BF16)
 
     stores = [
         [
@@ -337,25 +340,26 @@
 
 
 def upsample_kernel(
-    m0_hbm, m1_hbm, w_phase_hbm, o_ref, m0, m1, w_phase, turned, out, sems, load_sem
+    m0_hbm, m1_hbm, w_phase_hbm, o_ref, m0, m1, w_phase, d0, d1, turned, out, out_sem, load_sem
 ):
     loads = [
-        pltpu.make_async_copy(m0_hbm, m0, load_sem.at[4]),
-        pltpu.make_async_copy(m1_hbm, m1, load_sem.at[5]),
+        pltpu.make_async_copy(m0_hbm, m0, load_sem.at[6]),
+        pltpu.make_async_copy(m1_hbm, m1, load_sem.at[7]),
     ]
     phase_loads = [
-        pltpu.make_async_copy(w_phase_hbm.at[n], w_phase.at[n], load_sem.at[n]) for n in range(4)
+        pltpu.make_async_copy(w_phase_hbm.at[n], w_phase.at[n], load_sem.at[n]) for n in range(6)
     ]
     for load in loads + phase_loads:
         load.start()
     for load in loads:
         load.wait()
+    for difference, source in ((d0, m0), (d1, m1)):
+        difference[...] = (source[1:].astype(F32) - source[:7].astype(F32)).astype(BF16)
 
     def piece(group, n):
         first_iota, count = group
         lanes = pl.ds(pl.multiple_of((n * 30 + first_iota * 6) * 128, 128), count * 6 * 128)
-        sem = sems.at[n + (0 if first_iota == 0 else 16)]
-        return pltpu.make_async_copy(out.at[:, :, lanes], o_ref.at[:, :, lanes], sem)
+        return pltpu.make_async_copy(out.at[:, :, lanes], o_ref.at[:, :, lanes], out_sem)
 
     groups = ((0, 3), (3, 2))
     for group in groups:
@@ -363,25 +367,26 @@
         size = count * 16
         plain = slice(first_iota * 16, first_iota * 16 + size)
         after = slice(first_iota * 16 + 16, first_iota * 16 + 16 + size)
-        columns = (
-            ((m1, plain), (m0, plain), (m1, after)),
-            ((m0, plain), (m1, after), (m0, after)),
-        )
+        places = (((1, plain), (0, plain), (1, after)), ((0, plain), (1, after), (0, after)))
+
+        def product(pair, row, number, q, v, size=size, places=places):
+            taken = jnp.concatenate(
+                [
+                    pair[parity][row : row + 6, spot, :].reshape(6 * size, C)
+                    for parity, spot in places[q][v : v + 2]
+                ],
+                axis=1,
+            )
+            if first_iota == 0 and q == 0:
+                phase_loads[number].wait()
+            return dot_t(taken, w_phase[number])
+
         for q in range(2):
+            centre = [product((m0, m1), 1, v, q, v) for v in range(2)]
             for p in range(2):
-                halves = []
-                for v in range(2):
-                    if first_iota == 0 and q == 0:
-                        phase_loads[2 * p + v].wait()
-                    taken = jnp.concatenate(
-                        [
-                            source[p + i : p + i + 6, spot, :].reshape(6 * size, C)
-                            for i in range(2)
-                            for source, spot in columns[q][v : v + 2]
-                        ],
-                        axis=1,
-                    )
-                    halves.append(dot_t(taken, w_phase[2 * p + v]))
+                halves = [
+                    centre[v] + product((d0, d1), p, 2 + 2 * p + v, q, v) for v in range(2)
+                ]
                 whole = jnp.concatenate(halves, axis=1)
                 for i in range(6):
                     for at in range(count):
@@ -403,13 +408,7 @@
 
         lax.fori_loop(0, 16, write, 0)
 
-    for group in groups:
-
-        def finish(n, carry, group=group):
-            piece(group, n).wait()
-            return carry
-
-        lax.fori_loop(0, 16, finish, 0)
+    pltpu.make_async_copy(out, o_ref, out_sem).wait()
 
 
 def upsample(m0, m1, w_phase):
@@ -420,11 +419,12 @@
         out_specs=pl.BlockSpec(memory_space=pl.ANY),
         scratch_shapes=[
             *[pltpu.VMEM((8, 96, C), BF16)] * 2,
-            pltpu.VMEM((4, C_UP, 4 * C), BF16),
+            pltpu.VMEM((6, C_UP, 2 * C), BF16),
+            *[pltpu.VMEM((7, 96, C), BF16)] * 2,
             pltpu.VMEM((16 * PITCH, 128), F32),
             pltpu.VMEM((1, 12, 2 * 160 * C_UP), BF16),
-            pltpu.SemaphoreType.DMA((32,)),
-            pltpu.SemaphoreType.DMA((6,)),
+            pltpu.SemaphoreType.DMA,
+            pltpu.SemaphoreType.DMA((8,)),
         ],
         compiler_params=pltpu.CompilerParams(vmem_limit_bytes=UP_LIMIT * 2**20),
         name="upsample",
@@ -438,7 +438,7 @@
         out_shape=[
             jax.ShapeDtypeStruct((8, 96, C), BF16),
             jax.ShapeDtypeStruct((8, 96, C), BF16),
-            jax.ShapeDtypeStruct((4, C_UP, 4 * C), BF16),
+            jax.ShapeDtypeStruct((6, C_UP, 2 * C), BF16),
         ],
         in_specs=[pl.BlockSpec(memory_space=pl.ANY)] * 5,
         out_specs=[pl.BlockSpec(memory_space=pl.ANY)] * 3,
@@ -449,7 +449,7 @@
             pltpu.VMEM((27 * C, C), BF16),
             pltpu.VMEM((C_UP, 9 * C), BF16),
             pltpu.VMEM((768, 4 * C), BF16),
-            pltpu.VMEM((4, C_UP, 4 * C), BF16),
+            pltpu.VMEM((6, C_UP, 2 * C), BF16),
             pltpu.VMEM((2, 9 * C, C), BF16),
             *[pltpu.VMEM((8, 96, C), BF16)] * 2,
             pltpu.VMEM((BACK, 3 * TOKEN_ROW, 128), BF16),

time: 35.6 us -> 34.9 us (0.980)
  Pallas kernels: 35.3 us -> 34.6 us
    pallas_call x1, Pallas kernels: 8.3 us -> 7.54 us  [upsample(): pl.pallas_call(upsample_kernel, out_shape=jax.ShapeDtypeStruct((1, 12, 2...]
where the time goes in v5:
time: 34.9 us; the launch traced here: 34.7 us
  Pallas kernels  34.6 us (99%)
    pallas_call x1, Pallas kernels, on_device(): pl.pallas_call(functools.partial(mix_kernel, frames, rows), out_shape=[ja...  27 us
    pallas_call x1, Pallas kernels, upsample(): pl.pallas_call(upsample_kernel, out_shape=jax.ShapeDtypeStruct((1, 12, 2...  7.54 us

profile of v5, /device:TPU:97, one launch (start us, length us, event | category | flops | bytes accessed | tf_op | source)
XLA Modules:
  0.0 34.7 jit_solution(1436832463685050368)
XLA Ops:
  0.0 27.0 %mix.1 = (bf16[8,96,384]{2,1,0:T(8,128)(2,1)}, bf16[8,96,384]{2,1,0:T(8,128)(2,1)}, bf16[6,192,768]{2,1,0:T(8,128)(2,1)}) custom-call(bf16[120,128]{1,0:T(8,128)(2,1)} %x_ref.1, bf16[432,384]{1,0:T(8,128)(2,1)} %w_in_hbm.1, f32[384]{0:T(512)} %gain_hbm.1, bf16[10368,384]{1,0:T(8,128)(2,1)} %w_mid_hbm.1, bf16[192,3456]{1,0:T(8,128)(2,1)} %bitcast.1), custom_call_target="tpu_custom_call" | custom-call | tf_op jit(solution)/shard_map/mix/pallas_call | solution.py:436
  27.0 7.5 %upsample.1 = bf16[1,12,61440]{2,1,0:T(8,128)(2,1)} custom-call(bf16[8,96,384]{2,1,0:T(8,128)(2,1)} %get-tuple-element.8.m0_hbm, bf16[8,96,384]{2,1,0:T(8,128)(2,1)} %get-tuple-element.9.m1_hbm, bf16[6,192,768]{2,1,0:T(8,128)(2,1)} %get-tuple-element.10.w_phase_hbm), custom_call_target="tpu_custom_call" | custom-call | tf_op jit(solution)/shard_map/upsample/pallas_call | solution.py:415

commit v6 on v5

--- a/solution.py
+++ b/solution.py
@@ -321,13 +321,13 @@
                     put(target, (row,), q, iota, value)
                 stores[q][row].start()
 
-    for k, pieces in enumerate(((0, 1, 2), (3, 4, 5), (6, 7), (8, 9))):
-        accumulate(k, (1, 2), True)
-        normalize(0, result_c, pieces)
-    for k in range(3):
-        accumulate(k, (0,), False)
+    accumulate(0, (1, 2), True)
+    normalize(0, result_c)
+    accumulate(0, (0,), False)
+    for k in range(1, 3):
+        accumulate(k, (0, 1, 2), True)
     mix(0)
-    accumulate(3, (0,), False)
+    accumulate(3, (0, 1, 2), True)
     mix(1)
 
     for n, (k, d) in enumerate(peers()):
@@ -354,7 +354,7 @@
     for load in loads:
         load.wait()
     for difference, source in ((d0, m0), (d1, m1)):
-        difference[...] = (source[1:].astype(F32) - source[:7].astype(F32)).astype(BF16)
+        difference[...] = source[1:] - source[:7]
 
     def piece(group, n):
         first_iota, count = group

time: 34.9 us -> 34.5 us (0.989)
  Pallas kernels: 34.6 us -> 34.2 us
where the time goes in v6:
time: 34.5 us; the launch traced here: 34.4 us
  Pallas kernels  34.2 us (99%)
    pallas_call x1, Pallas kernels, on_device(): pl.pallas_call(functools.partial(mix_kernel, frames, rows), out_shape=[ja...  26.8 us
    pallas_call x1, Pallas kernels, upsample(): pl.pallas_call(upsample_kernel, out_shape=jax.ShapeDtypeStruct((1, 12, 2...  7.44 us

profile of v6, /device:TPU:97, one launch (start us, length us, event | category | flops | bytes accessed | tf_op | source)
XLA Modules:
  0.0 34.4 jit_solution(4738012727336538704)
XLA Ops:
  0.0 26.8 %mix.1 = (bf16[8,96,384]{2,1,0:T(8,128)(2,1)}, bf16[8,96,384]{2,1,0:T(8,128)(2,1)}, bf16[6,192,768]{2,1,0:T(8,128)(2,1)}) custom-call(bf16[120,128]{1,0:T(8,128)(2,1)} %x_ref.1, bf16[432,384]{1,0:T(8,128)(2,1)} %w_in_hbm.1, f32[384]{0:T(512)} %gain_hbm.1, bf16[10368,384]{1,0:T(8,128)(2,1)} %w_mid_hbm.1, bf16[192,3456]{1,0:T(8,128)(2,1)} %bitcast.1), custom_call_target="tpu_custom_call" | custom-call | tf_op jit(solution)/shard_map/mix/pallas_call | solution.py:436
  26.8 7.4 %upsample.1 = bf16[1,12,61440]{2,1,0:T(8,128)(2,1)} custom-call(bf16[8,96,384]{2,1,0:T(8,128)(2,1)} %get-tuple-element.8.m0_hbm, bf16[8,96,384]{2,1,0:T(8,128)(2,1)} %get-tuple-element.9.m1_hbm, bf16[6,192,768]{2,1,0:T(8,128)(2,1)} %get-tuple-element.10.w_phase_hbm), custom_call_target="tpu_custom_call" | custom-call | tf_op jit(solution)/shard_map/upsample/pallas_call | solution.py:415

commit v7 on v6

--- a/solution.py
+++ b/solution.py
@@ -264,7 +264,8 @@
                 put(target, (g, 3, pair), q, iota, odd - next_odd)
                 even, odd = next_even, next_odd
 
-    arrive((0, 1, 2))
+    arrive((0, 1))
+    arrive((2,))
     convolve(2, result_a)
     arrive((3,))
     convolve(1, result_b)
@@ -421,7 +422,7 @@
             *[pltpu.VMEM((8, 96, C), BF16)] * 2,
             pltpu.VMEM((6, C_UP, 2 * C), BF16),
             *[pltpu.VMEM((7, 96, C), BF16)] * 2,
-            pltpu.VMEM((16 * PITCH, 128), F32),
+            pltpu.VMEM((17 * PITCH, 128), F32),
             pltpu.VMEM((1, 12, 2 * 160 * C_UP), BF16),
             pltpu.SemaphoreType.DMA,
             pltpu.SemaphoreType.DMA((8,)),
@@ -455,7 +456,7 @@
             pltpu.VMEM((BACK, 3 * TOKEN_ROW, 128), BF16),
             pltpu.VMEM((BACK + 1, 2 * TOKEN_ROW, 128), BF16),
             pltpu.VMEM((BACK + 1, 2 * TOKEN_ROW, 128), BF16),
-            pltpu.VMEM(((BACK + 1) * 7 * HALF, 128), F32),
+            pltpu.VMEM(((BACK + 1) * 7 * HALF + 16, 128), F32),
             pltpu.VMEM((BACK + 1, 7 * HALF, 128), BF16),
             pltpu.VMEM((BACK + 1, 5 * HALF, 256), BF16),
             pltpu.VMEM((2, 10, HALF, C), BF16),

time: 34.5 us -> 34.7 us (level)
  no operation moved by 1% of the time
where the time goes in v7:
time: 34.7 us; the launch traced here: 34.6 us
  Pallas kernels  34.4 us (99%)
    pallas_call x1, Pallas kernels, on_device(): pl.pallas_call(functools.partial(mix_kernel, frames, rows), out_shape=[ja...  27 us
    pallas_call x1, Pallas kernels, upsample(): pl.pallas_call(upsample_kernel, out_shape=jax.ShapeDtypeStruct((1, 12, 2...  7.44 us

profile of v7, /device:TPU:97, one launch (start us, length us, event | category | flops | bytes accessed | tf_op | source)
XLA Modules:
  0.0 34.6 jit_solution(6271381591480957061)
XLA Ops:
  0.0 27.0 %mix.1 = (bf16[8,96,384]{2,1,0:T(8,128)(2,1)}, bf16[8,96,384]{2,1,0:T(8,128)(2,1)}, bf16[6,192,768]{2,1,0:T(8,128)(2,1)}) custom-call(bf16[120,128]{1,0:T(8,128)(2,1)} %x_ref.1, bf16[432,384]{1,0:T(8,128)(2,1)} %w_in_hbm.1, f32[384]{0:T(512)} %gain_hbm.1, bf16[10368,384]{1,0:T(8,128)(2,1)} %w_mid_hbm.1, bf16[192,3456]{1,0:T(8,128)(2,1)} %bitcast.1), custom_call_target="tpu_custom_call" | custom-call | tf_op jit(solution)/shard_map/mix/pallas_call | solution.py:437
  27.0 7.4 %upsample.1 = bf16[1,12,61440]{2,1,0:T(8,128)(2,1)} custom-call(bf16[8,96,384]{2,1,0:T(8,128)(2,1)} %get-tuple-element.8.m0_hbm, bf16[8,96,384]{2,1,0:T(8,128)(2,1)} %get-tuple-element.9.m1_hbm, bf16[6,192,768]{2,1,0:T(8,128)(2,1)} %get-tuple-element.10.w_phase_hbm), custom_call_target="tpu_custom_call" | custom-call | tf_op jit(solution)/shard_map/upsample/pallas_call | solution.py:416

commit v8 on v7

--- a/solution.py
+++ b/solution.py
@@ -214,10 +214,10 @@
     at = lax.broadcasted_iota(jnp.int32, (16, C), 0)
 
     def shifted_right(values):
-        return jnp.where(at == 0, 0.0, pltpu.roll(values, 1, 0)).astype(BF16)
+        return jnp.where(at == 0, 0.0, pltpu.roll(values.astype(F32), 1, 0)).astype(BF16)
 
     def shifted_left(values):
-        return jnp.where(at == 15, 0.0, pltpu.roll(values, 15, 0)).astype(BF16)
+        return jnp.where(at == 15, 0.0, pltpu.roll(values.astype(F32), 15, 0)).astype(BF16)
 
     def put(target, spot, q, iota, value):
         start = (iota + q) * 16
@@ -247,7 +247,7 @@
         if row >= 8:
             scale = scale * bottom
         value = value * scale * half_gain
-        return value + value * jnp.tanh(value)
+        return (value + value * jnp.tanh(value)).astype(BF16)
 
     def normalize(g, result, pieces=range(10)):
         for piece in pieces:

time: 34.7 us -> 34.6 us (level)
  no operation moved by 1% of the time
where the time goes in v8:
time: 34.6 us; the launch traced here: 34.5 us
  Pallas kernels  34.3 us (99%)
    pallas_call x1, Pallas kernels, on_device(): pl.pallas_call(functools.partial(mix_kernel, frames, rows), out_shape=[ja...  26.9 us
    pallas_call x1, Pallas kernels, upsample(): pl.pallas_call(upsample_kernel, out_shape=jax.ShapeDtypeStruct((1, 12, 2...  7.46 us

profile of v8, /device:TPU:97, one launch (start us, length us, event | category | flops | bytes accessed | tf_op | source)
XLA Modules:
  0.0 34.5 jit_solution(10128597477592810156)
XLA Ops:
  0.0 26.9 %mix.1 = (bf16[8,96,384]{2,1,0:T(8,128)(2,1)}, bf16[8,96,384]{2,1,0:T(8,128)(2,1)}, bf16[6,192,768]{2,1,0:T(8,128)(2,1)}) custom-call(bf16[120,128]{1,0:T(8,128)(2,1)} %x_ref.1, bf16[432,384]{1,0:T(8,128)(2,1)} %w_in_hbm.1, f32[384]{0:T(512)} %gain_hbm.1, bf16[10368,384]{1,0:T(8,128)(2,1)} %w_mid_hbm.1, bf16[192,3456]{1,0:T(8,128)(2,1)} %bitcast.1), custom_call_target="tpu_custom_call" | custom-call | tf_op jit(solution)/shard_map/mix/pallas_call | solution.py:437
  26.9 7.5 %upsample.1 = bf16[1,12,61440]{2,1,0:T(8,128)(2,1)} custom-call(bf16[8,96,384]{2,1,0:T(8,128)(2,1)} %get-tuple-element.8.m0_hbm, bf16[8,96,384]{2,1,0:T(8,128)(2,1)} %get-tuple-element.9.m1_hbm, bf16[6,192,768]{2,1,0:T(8,128)(2,1)} %get-tuple-element.10.w_phase_hbm), custom_call_target="tpu_custom_call" | custom-call | tf_op jit(solution)/shard_map/upsample/pallas_call | solution.py:416
